TPU v7x, 512 devices: a whole 4x8x8 slice. The times are simulated.
512 devices in a mesh: dp: 32 (over y, x), tensor: 16 (over z, core).
Axes of the slice: x: 4, y: 8, z: 8, core: 2. Of those that a mesh axis runs over, the one named last changes fastest.
Arguments:
- hidden_in: bfloat16 [2048, 12288], P('dp'), may hold values from -6 to 6
- norm_gain: bfloat16 [12288], replicated, may hold values from 0.099609375 to 1.8984375
- norm_shift: bfloat16 [12288], replicated, may hold values from -3 to 3
- up_weight: bfloat16 [12288, 24576], P('dp', 'tensor'), may hold values from -0.0546875 to 0.0546875
- up_bias: bfloat16 [24576], P('tensor'), may hold values from -3 to 3
- down_weight: bfloat16 [24576, 12288], P('tensor', 'dp'), may hold values from -0.09375 to 0.09375
- down_bias: bfloat16 [12288], P('tensor'), may hold values from -3 to 3
- active: int32 [64, 16, 4], P(None, 'tensor'), may hold values from 0 to 11, as said below
- counts: int32 [64, 16], P(None, 'tensor'), may hold values from 1 to 4, as said below
Outputs:
- hidden_out: bfloat16 [2048, 12288], P('dp', 'tensor')
Inputs may be any that keep to these rules, and one draw needn't show every extreme that they name: The 4 entries of each list are distinct; only the first counts entries are active. `counts`: every row group has a list with all 4 slots valid.
All inputs are finite; a program needn't handle non-finite values.
Results may differ from a plain program's by a relative error of at most 0.022.
Values may be sent and summed in bfloat16 or wider, within the bound.
No kernel may reach another device: no remote copies, remote signals or barrier semaphores. Data moves between devices by JAX's collectives and lax.ppermute only.
A program may use at most 64 MiB of HBM per device.

v0:
```python
import math
import jax
import jax.numpy as jnp
from jax import lax
from jax.sharding import PartitionSpec as P

BLOCK = 128
GROUP = 32


def in_blocks(step_fn, arrays):
    total = arrays[0].shape[0]
    per = math.gcd(total, 8)
    stacked = tuple((item.reshape((total // per, per) + item.shape[1:]) for item in arrays))
    result = lax.map(step_fn, stacked)
    return result.reshape((total,) + result.shape[2:])


def select_up(rows, ids, up_table):
    ngroups, slots = ids.shape
    grouped = rows.reshape(ngroups, -1, rows.shape[1])

    def step(pair):
        block_rows, block_ids = pair
        chosen = jnp.take(up_table, block_ids, axis=1)
        return jnp.einsum("grd,dgcb->grcb", block_rows, chosen, preferred_element_type=jnp.float32)

    result = in_blocks(step, (grouped, ids))
    return result.reshape(rows.shape[0], slots * up_table.shape[2])


def select_down(act, ids, down_table):
    ngroups, slots = ids.shape
    grouped = act.reshape(ngroups, -1, slots, down_table.shape[1])

    def step(pair):
        block_act, block_ids = pair
        chosen = jnp.take(down_table, block_ids, axis=0)
        return jnp.einsum("grcb,gcbd->grd", block_act, chosen, preferred_element_type=jnp.float32)

    result = in_blocks(step, (grouped, ids))
    return result.reshape(act.shape[0], down_table.shape[2])


def activate(pre, ids, valid, bias_table):
    ngroups, slots = ids.shape
    own = bias_table.shape[0]
    onehot = (ids[:, :, None] == jnp.arange(own, dtype=jnp.int32)[None, None, :]).astype(
        jnp.float32
    )
    bias_sel = jnp.einsum("gco,ob->gcb", onehot, bias_table, precision=lax.Precision.HIGHEST)
    mask = (jnp.arange(slots, dtype=jnp.int32)[None, :] < valid[:, None]).astype(jnp.float32)
    shaped = pre.reshape(ngroups, -1, slots, bias_table.shape[1])
    result = jnp.maximum(shaped + bias_sel[:, None], 0.0) * mask[:, None, :, None]
    return result.astype(jnp.bfloat16).reshape(pre.shape)


def body(
    hidden_in, norm_gain, norm_shift, up_weight, up_bias, down_weight, down_bias, active, counts
):
    row_dev = hidden_in.shape[0]
    values = hidden_in.astype(jnp.float32)
    center = values - jnp.mean(values, axis=-1, keepdims=True)
    spread = jnp.mean(center * center, axis=-1, keepdims=True)
    normed = (
        center * lax.rsqrt(spread + 1e-05) * norm_gain.astype(jnp.float32)
        + norm_shift.astype(jnp.float32)
    ).astype(jnp.bfloat16)
    columns = lax.all_to_all(normed, "dp", split_axis=1, concat_axis=0, tiled=True)
    d_part = up_weight.shape[0]
    own = up_weight.shape[1] // BLOCK
    up_table = up_weight.reshape(d_part, own, BLOCK)
    down_table = down_weight.reshape(own, BLOCK, d_part)
    bias_table = up_bias.astype(jnp.float32).reshape(own, BLOCK)
    ids = active[:, 0, :]
    valid = counts[:, 0]
    pre_own = lax.psum_scatter(
        select_up(columns, ids, up_table).astype(jnp.bfloat16),
        "dp",
        scatter_dimension=0,
        tiled=True,
    ).astype(jnp.float32)
    per_dev = row_dev // GROUP
    first = lax.axis_index("dp") * per_dev
    own_ids = lax.dynamic_slice_in_dim(ids, first, per_dev, 0)
    own_valid = lax.dynamic_slice_in_dim(valid, first, per_dev, 0)
    act_own = activate(pre_own, own_ids, own_valid, bias_table)
    act = lax.all_gather(act_own, "dp", axis=0, tiled=True)
    branch = select_down(act, ids, down_table)
    branch = branch.astype(jnp.bfloat16)
    returned = lax.all_to_all(branch, "dp", split_axis=0, concat_axis=1, tiled=True)
    summed = lax.psum_scatter(
        returned.astype(jnp.float32).astype(jnp.bfloat16), "tensor", scatter_dimension=1, tiled=True
    ).astype(jnp.float32)
    width = summed.shape[1]
    resid = lax.dynamic_slice_in_dim(hidden_in, lax.axis_index("tensor") * width, width, 1).astype(
        jnp.float32
    )
    return (resid + summed + down_bias.astype(jnp.float32)).astype(jnp.bfloat16)


def solution(mesh):
    placed = (
        P("dp", None),
        P(),
        P(),
        P("dp", "tensor"),
        P("tensor"),
        P("tensor", "dp"),
        P("tensor"),
        P(None, "tensor", None),
        P(None, "tensor"),
    )
    return jax.shard_map(
        body, mesh=mesh, in_specs=placed, out_specs=P("dp", "tensor"), check_vma=False
    )
```

profile of v0, /device:TPU:6, one launch (start us, length us, event | category | flops | bytes accessed | tf_op | source)
XLA Modules:
  0.0 595.1 jit_solution(5143126974400507887)
XLA Ops:
  6.5 1.8 convert_reduce_fusion
  8.4 0.6 fusion.28
  9.1 0.6 fusion.31
  9.8 1.4 copy.71
  11.2 10.4 %all-to-all-start = ((bf16[64,32,384]{2,0,1:T(8,128)(2,1)}), bf16[64,32,384]{2,0,1:T(8,128)(2,1)}, u32[]{:S(2)}, u32[]{:S(2)}) async-start(bf16[64,32,384]{2,0,1:T(8,128)(2,1)} %bitcast.85), calls=%async_computation | async-start | bytes 3145728 | tf_op jit(solution)/shard_map/all_to_all | solution.py:69
  21.7 1.4 copy.48
  23.2 1.7 copy.50
  24.9 36.1 %all-to-all-done = bf16[64,32,384]{2,0,1:T(8,128)(2,1)} async-done(((bf16[64,32,384]{2,0,1:T(8,128)(2,1)}), bf16[64,32,384]{2,0,1:T(8,128)(2,1)}, u32[]{:S(2)}, u32[]{:S(2)}) %all-to-all-start) | async-done | bytes 1572896 | tf_op jit(solution)/shard_map/all_to_all | solution.py:69
  60.9 51.3 %while.20 = (s32[]{:T(128)}, bf16[8,8,32,4,128]{4,2,3,1,0:T(8,128)(2,1)}, bf16[8,8,32,384]{3,2,1,0:T(8,128)(2,1)}, s32[8,8,4]{1,2,0:T(4,128)S(1)}, bf16[384,12,128]{2,0,1:T(8,128)(2,1)S(1)}, /*index=5*/s32[]{:T(128)}) while((s32[]{:T(128)}, bf16[8,8,32,4,128]{4,2,3,1,0:T(8,128)(2,1)}, bf16[8,8,32,384]{3,2,1,0:T(8,128)(2,1)}, ...), condition=%wide.region_3.4_spmd, body=%wide.region_2.3_spmd.sunk | while | flops 102237472 | bytes 10164557 | solution.py:15
  61.1 2.6 gather_fusion
  63.8 3.5 fusion.45
  67.5 2.6 gather_fusion
  70.1 0.1 copy.78
  70.2 3.5 fusion.45
  73.9 2.6 gather_fusion
  76.6 3.6 fusion.45
  80.3 2.6 gather_fusion
  83.0 3.5 fusion.45
  86.7 2.6 gather_fusion
  89.4 3.5 fusion.45
  93.1 2.6 gather_fusion
  95.8 3.6 fusion.45
  99.6 2.6 gather_fusion
  102.3 3.5 fusion.45
  106.0 2.6 gather_fusion
  108.6 0.1 copy.78
  108.7 3.5 fusion.45
  112.2 2.7 copy.51
  114.9 1.7 copy.70
  116.8 0.4 copy-done.8
  117.4 0.2 fusion.34
  117.6 219.8 %reduce-scatter.3.cloned.1.call-done = bf16[64,512]{1,0:T(8,128)(2,1)} async-done(((bf16[2048,512]{1,0:T(8,128)(2,1)}), bf16[64,512]{1,0:T(8,128)(2,1)}) %reduce-scatter.3.cloned.1.call-update) | async-done | bytes 65552 | tf_op jit(solution)/shard_map/reduce_scatter | solution.py:77
  337.5 1.5 fusion.32
  339.1 83.5 %all-gather.2.cloned.1.call-done = bf16[2048,512]{1,0:T(8,128)(2,1)} async-done(((bf16[64,512]{1,0:T(8,128)(2,1)}), bf16[2048,512]{1,0:T(8,128)(2,1)}) %all-gather.2.cloned.1.call-update) | async-done | bytes 2097168 | tf_op jit(solution)/shard_map/all_gather | solution.py:88
  422.6 4.0 reshape_reshape.9
  426.6 57.6 %while.21 = (s32[]{:T(128)}, bf16[8,8,32,384]{3,2,1,0:T(8,128)(2,1)}, bf16[8,8,32,4,128]{4,3,2,1,0:T(4,128)(2,1)}, s32[8,8,4]{1,2,0:T(4,128)S(1)}, bf16[12,128,384]{2,1,0:T(8,128)(2,1)S(1)}, /*index=5*/s32[]{:T(128)}) while((s32[]{:T(128)}, bf16[8,8,32,384]{3,2,1,0:T(8,128)(2,1)}, bf16[8,8,32,4,128]{4,3,2,1,0:T(4,128)(2,1)}, ...), condition=%wide.region_6.7_spmd, body=%wide.region_5.6_spmd.sunk | while | flops 102237472 | bytes 10622801 | solution.py:15
  426.7 2.6 gather_fusion.1
  429.5 1.0 constant_dynamic-slice_fusion.4
  430.5 3.3 fusion.47
  433.9 2.6 gather_fusion.1
  436.7 1.0 constant_dynamic-slice_fusion.4
  437.7 3.3 fusion.47
  441.2 2.6 gather_fusion.1
  443.9 1.0 constant_dynamic-slice_fusion.4
  444.9 3.3 fusion.47
  448.4 2.6 gather_fusion.1
  451.1 1.0 constant_dynamic-slice_fusion.4
  452.1 3.3 fusion.47
  455.6 2.6 gather_fusion.1
  458.3 1.0 constant_dynamic-slice_fusion.4
  459.3 3.2 fusion.47
  462.8 2.6 gather_fusion.1
  465.5 1.0 constant_dynamic-slice_fusion.4
  466.5 3.3 fusion.47
  470.0 2.6 gather_fusion.1
  472.7 1.0 constant_dynamic-slice_fusion.4
  473.7 3.2 fusion.47
  477.1 2.6 gather_fusion.1
  479.9 1.0 constant_dynamic-slice_fusion.4
  480.9 3.3 fusion.47
  484.2 42.5 %all_to_all.32 = bf16[32,64,384]{2,1,0:T(8,128)(2,1)S(1)} all-to-all(bf16[32,64,384]{2,1,0:T(8,128)(2,1)} %bitcast.117), channel_id=1, replica_groups=mesh['dp'=32,'tensor'=16] {'dp'}, dimensions={0} | all-to-all | bytes 3145728 | tf_op jit(solution)/shard_map/all_to_all | solution.py:91
  526.7 1.3 copy.60
  528.0 59.0 %reduce-scatter.5.cloned.1.call-done = bf16[64,768]{1,0:T(8,128)(2,1)} async-done(((bf16[64,12288]{1,0:T(8,128)(2,1)}), bf16[64,768]{1,0:T(8,128)(2,1)}) %reduce-scatter.5.cloned.1.call-update) | async-done | bytes 98320 | tf_op jit(solution)/shard_map/reduce_scatter | solution.py:92
  587.0 1.6 add_convert_fusion
  (132 shorter events, 5.1 us)
Async XLA Ops:
  6.5 110.9 %copy-start = (bf16[1536]{0:T(1024)(128)(2,1)S(1)}, bf16[1536]{0:T(1024)(128)(2,1)}, u32[]{:S(2)}) copy-start(bf16[1536]{0:T(1024)(128)(2,1)} %param.17) | copy-start | bytes 9220
  6.5 1.9 copy-start.2
  6.5 2.5 copy-start.4
  6.5 2.5 copy-start.5
  11.2 10.4 %copy-start.6 = (s32[64,1,4]{0,2,1:T(4,128)S(1)}, s32[64,1,4]{0,2,1:T(4,128)}, u32[]{:S(2)}) copy-start(s32[64,1,4]{0,2,1:T(4,128)} %param.20) | copy-start | bytes 3076
  11.2 10.5 %copy-start.3 = (bf16[384,1536]{1,0:T(8,128)(2,1)S(1)}, bf16[384,1536]{1,0:T(8,128)(2,1)}, u32[]{:S(2)}) copy-start(bf16[384,1536]{1,0:T(8,128)(2,1)} %param.16) | copy-start | bytes 3538948
  11.2 49.7 %all-to-all-start = ((bf16[64,32,384]{2,0,1:T(8,128)(2,1)}), bf16[64,32,384]{2,0,1:T(8,128)(2,1)}, u32[]{:S(2)}, u32[]{:S(2)}) async-start(bf16[64,32,384]{2,0,1:T(8,128)(2,1)} %bitcast.85), calls=%async_computation | async-start | bytes 3145728 | tf_op jit(solution)/shard_map/all_to_all | solution.py:69
  21.6 315.8 %reduce-scatter.3.cloned.1.call-start = ((), (), s32[]{:S(2)}) async-start(), calls=%async_computation.4 | async-start | bytes 2162688 | tf_op jit(solution)/shard_map/reduce_scatter | solution.py:77
  116.6 0.7 copy-start.8
  116.6 306.0 %all-gather.2.cloned.1.call-start = ((), (), s32[]{:S(2)}) async-start(), calls=%async_computation.5 | async-start | bytes 2162688 | tf_op jit(solution)/shard_map/all_gather | solution.py:88
  339.0 248.0 %reduce-scatter.5.cloned.1.call-start = ((), (), s32[]{:S(2)}) async-start(), calls=%async_computation.6 | async-start | bytes 1671168 | tf_op jit(solution)/shard_map/reduce_scatter | solution.py:92
  339.1 87.5 %copy-start.1 = (bf16[1536,384]{1,0:T(8,128)(2,1)S(1)}, bf16[1536,384]{1,0:T(8,128)(2,1)}, u32[]{:S(2)}) copy-start(bf16[1536,384]{1,0:T(8,128)(2,1)} %param.18) | copy-start | bytes 3538948
  526.7 1.4 copy-start.7
Sparse Core Ops, SparseCore 0:
  116.7 220.6 reduce-scatter.2
  341.0 81.5 all-gather.1
  528.1 58.8 reduce-scatter.4
where the time goes:
time: 596 us; the launch traced here: 595 us
  waiting for transfers between devices  398 us (67%)
  local copies, waits for them, and re-layouts  69.3 us (12%)
  matrix products  54.5 us (9%)
  blocking collectives  42.5 us (7%)
  between operations  13.3 us (2%)
  starting transfers between devices  10.5 us (2%)
  other arithmetic  6.56 us (1%)
    reduce_scatter x1, waiting for transfers between devices, body(): lax.psum_scatter(select_up(columns, ids, up_table).astype(jnp.bfloat16),...  220 us
    all_gather x1, waiting for transfers between devices, body(): act = lax.all_gather(act_own, 'dp', axis=0, tiled=True)  83.5 us
    reduce_scatter x1, waiting for transfers between devices, body(): lax.psum_scatter(returned.astype(jnp.float32).astype(jnp.bfloat16), 'tens...  59 us
    all_to_all x1, blocking collectives, body(): lax.all_to_all(branch, 'dp', split_axis=0, concat_axis=1, tiled=True)  42.5 us
    all_to_all x1, waiting for transfers between devices, body(): lax.all_to_all(normed, 'dp', split_axis=1, concat_axis=0, tiled=True)  36.1 us
    dot_general x8, matrix products, step(): jnp.einsum('grd,dgcb->grcb', block_rows, chosen, preferred_element_type=j...  28.3 us
    dot_general x8, matrix products, step(): jnp.einsum('grcb,gcbd->grd', block_act, chosen, preferred_element_type=jn...  26 us
    gather x8, local copies, waits for them, and re-layouts, step(): chosen = jnp.take(down_table, block_ids, axis=0)  20.9 us
  transfers between devices with their start and end apart: 4, of which 4 were waited for; matrix products, arithmetic and copies ran while one was open for 1% of the time, Pallas kernels for 0%

commit v1 on v0

--- a/solution.py
+++ b/solution.py
@@ -85,7 +85,10 @@
     own_ids = lax.dynamic_slice_in_dim(ids, first, per_dev, 0)
     own_valid = lax.dynamic_slice_in_dim(valid, first, per_dev, 0)
     act_own = activate(pre_own, own_ids, own_valid, bias_table)
-    act = lax.all_gather(act_own, "dp", axis=0, tiled=True)
+    size = lax.axis_size("dp")
+    blocks = jnp.stack([act_own for _ in range(size)])
+    blocks = lax.all_to_all(blocks, "dp", split_axis=0, concat_axis=0)
+    act = jnp.concatenate(blocks, axis=0)
     branch = select_down(act, ids, down_table)
     branch = branch.astype(jnp.bfloat16)
     returned = lax.all_to_all(branch, "dp", split_axis=0, concat_axis=1, tiled=True)

time: 596 us -> 566 us (0.950)
  waiting for transfers between devices: 398 us -> 359 us
  starting transfers between devices: 10.5 us -> 18.7 us
    all_gather x1 -> x0, waiting for transfers between devices: 83.5 us -> none  [body(): act = lax.all_gather(act_own, 'dp', axis=0, tiled=True)]
    all_to_all x0 -> x1, waiting for transfers between devices: none -> 44.6 us  [body(): blocks = lax.all_to_all(blocks, 'dp', split_axis=0, concat_axis=0)]
    all_to_all x0 -> x1, starting transfers between devices: none -> 8.22 us  [body(): blocks = lax.all_to_all(blocks, 'dp', split_axis=0, concat_axis=0)]
where the time goes in v1:
time: 566 us; the launch traced here: 565 us
  waiting for transfers between devices  359 us (63%)
  local copies, waits for them, and re-layouts  71 us (13%)
  matrix products  54.4 us (10%)
  blocking collectives  41.9 us (7%)
  starting transfers between devices  18.7 us (3%)
  between operations  13.6 us (2%)
  other arithmetic  5.93 us (1%)
    reduce_scatter x1, waiting for transfers between devices, body(): lax.psum_scatter(select_up(columns, ids, up_table).astype(jnp.bfloat16),...  220 us
    reduce_scatter x1, waiting for transfers between devices, body(): lax.psum_scatter(returned.astype(jnp.float32).astype(jnp.bfloat16), 'tens...  58.7 us
    all_to_all x1, waiting for transfers between devices, body(): blocks = lax.all_to_all(blocks, 'dp', split_axis=0, concat_axis=0)  44.6 us
    all_to_all x1, blocking collectives, body(): lax.all_to_all(branch, 'dp', split_axis=0, concat_axis=1, tiled=True)  41.9 us
    all_to_all x1, waiting for transfers between devices, body(): lax.all_to_all(normed, 'dp', split_axis=1, concat_axis=0, tiled=True)  36.1 us
    dot_general x8, matrix products, step(): jnp.einsum('grd,dgcb->grcb', block_rows, chosen, preferred_element_type=j...  28.3 us
    dot_general x8, matrix products, step(): jnp.einsum('grcb,gcbd->grd', block_act, chosen, preferred_element_type=jn...  26 us
    gather x8, local copies, waits for them, and re-layouts, step(): chosen = jnp.take(down_table, block_ids, axis=0)  21 us
  transfers between devices with their start and end apart: 4, of which 4 were waited for; matrix products, arithmetic and copies ran while one was open for 1% of the time, Pallas kernels for 0%

profile of v1, /device:TPU:6, one launch (start us, length us, event | category | flops | bytes accessed | tf_op | source)
XLA Modules:
  0.0 564.8 jit_solution(16889448706743001342)
XLA Ops:
  6.5 1.8 convert_reduce_fusion
  8.4 0.6 fusion.28
  9.1 0.6 fusion.31
  9.8 1.4 copy.71
  11.2 10.4 %all-to-all-start = ((bf16[64,32,384]{2,0,1:T(8,128)(2,1)}), bf16[64,32,384]{2,0,1:T(8,128)(2,1)}, u32[]{:S(2)}, u32[]{:S(2)}) async-start(bf16[64,32,384]{2,0,1:T(8,128)(2,1)} %bitcast.85), calls=%async_computation | async-start | bytes 3145728 | tf_op jit(solution)/shard_map/all_to_all | solution.py:69
  21.7 1.4 copy.48
  23.2 1.7 copy.50
  24.9 36.1 %all-to-all-done = bf16[64,32,384]{2,0,1:T(8,128)(2,1)} async-done(((bf16[64,32,384]{2,0,1:T(8,128)(2,1)}), bf16[64,32,384]{2,0,1:T(8,128)(2,1)}, u32[]{:S(2)}, u32[]{:S(2)}) %all-to-all-start) | async-done | bytes 1572896 | tf_op jit(solution)/shard_map/all_to_all | solution.py:69
  60.9 51.3 %while.20 = (s32[]{:T(128)}, bf16[8,8,32,4,128]{4,2,3,1,0:T(8,128)(2,1)}, bf16[8,8,32,384]{3,2,1,0:T(8,128)(2,1)}, s32[8,8,4]{1,2,0:T(4,128)S(1)}, bf16[384,12,128]{2,0,1:T(8,128)(2,1)S(1)}, /*index=5*/s32[]{:T(128)}) while((s32[]{:T(128)}, bf16[8,8,32,4,128]{4,2,3,1,0:T(8,128)(2,1)}, bf16[8,8,32,384]{3,2,1,0:T(8,128)(2,1)}, ...), condition=%wide.region_3.4_spmd, body=%wide.region_2.3_spmd.sunk | while | flops 102237472 | bytes 10164557 | solution.py:15
  61.1 2.6 gather_fusion
  63.8 3.5 fusion.45
  67.5 2.6 gather_fusion
  70.2 3.5 fusion.45
  73.9 2.6 gather_fusion
  76.6 3.5 fusion.45
  80.3 2.6 gather_fusion
  83.0 3.5 fusion.45
  86.7 2.6 gather_fusion
  89.4 3.5 fusion.45
  93.1 2.6 gather_fusion
  95.8 3.6 fusion.45
  99.6 2.6 gather_fusion
  102.3 3.5 fusion.45
  106.0 2.6 gather_fusion
  108.7 3.5 fusion.45
  112.2 2.7 copy.51
  114.9 1.7 copy.70
  116.8 0.5 copy-done.8
  117.4 0.2 fusion.34
  117.6 219.8 %reduce-scatter.3.cloned.1.call-done = bf16[64,512]{1,0:T(8,128)(2,1)} async-done(((bf16[2048,512]{1,0:T(8,128)(2,1)}), bf16[64,512]{1,0:T(8,128)(2,1)}) %reduce-scatter.3.cloned.1.call-update) | async-done | bytes 65552 | tf_op jit(solution)/shard_map/reduce_scatter | solution.py:77
  337.5 0.9 fusion.32
  338.3 1.6 stack.3
  339.9 8.2 %all-to-all-start.1 = ((bf16[32,64,512]{2,1,0:T(8,128)(2,1)}), bf16[32,64,512]{2,1,0:T(8,128)(2,1)}, u32[]{:S(2)}, u32[]{:S(2)}) async-start(bf16[32,64,512]{2,1,0:T(8,128)(2,1)} %stack.3), calls=%async_computation.2 | async-start | bytes 4194304 | tf_op jit(solution)/shard_map/all_to_all | solution.py:90
  348.2 44.6 %all-to-all-done.1 = bf16[32,64,512]{2,1,0:T(8,128)(2,1)} async-done(((bf16[32,64,512]{2,1,0:T(8,128)(2,1)}), bf16[32,64,512]{2,1,0:T(8,128)(2,1)}, u32[]{:S(2)}, u32[]{:S(2)}) %all-to-all-start.1) | async-done | bytes 2097184 | tf_op jit(solution)/shard_map/all_to_all | solution.py:90
  392.8 4.0 reshape_reshape_reshape.3
  396.8 57.6 %while.21 = (s32[]{:T(128)}, bf16[8,8,32,384]{3,2,1,0:T(8,128)(2,1)}, bf16[8,8,32,4,128]{4,3,2,1,0:T(4,128)(2,1)}, s32[8,8,4]{1,2,0:T(4,128)S(1)}, bf16[12,128,384]{2,1,0:T(8,128)(2,1)S(1)}, /*index=5*/s32[]{:T(128)}) while((s32[]{:T(128)}, bf16[8,8,32,384]{3,2,1,0:T(8,128)(2,1)}, bf16[8,8,32,4,128]{4,3,2,1,0:T(4,128)(2,1)}, ...), condition=%wide.region_6.7_spmd, body=%wide.region_5.6_spmd.sunk | while | flops 102237472 | bytes 10622801 | solution.py:15
  397.0 2.6 gather_fusion.1
  399.7 1.0 constant_dynamic-slice_fusion.4
  400.7 3.2 fusion.47
  404.2 2.6 gather_fusion.1
  406.9 1.0 constant_dynamic-slice_fusion.4
  407.9 3.3 fusion.47
  411.4 2.6 gather_fusion.1
  414.1 1.0 constant_dynamic-slice_fusion.4
  415.2 3.3 fusion.47
  418.6 2.6 gather_fusion.1
  421.3 1.0 constant_dynamic-slice_fusion.4
  422.4 3.2 fusion.47
  425.8 2.6 gather_fusion.1
  428.5 1.0 constant_dynamic-slice_fusion.4
  429.6 3.2 fusion.47
  433.0 2.6 gather_fusion.1
  435.7 1.0 constant_dynamic-slice_fusion.4
  436.8 3.3 fusion.47
  440.2 2.6 gather_fusion.1
  442.9 1.0 constant_dynamic-slice_fusion.4
  444.0 3.2 fusion.47
  447.4 2.6 gather_fusion.1
  450.1 1.0 constant_dynamic-slice_fusion.4
  451.2 3.2 fusion.47
  454.4 41.9 %all_to_all.37 = bf16[32,64,384]{2,1,0:T(8,128)(2,1)S(1)} all-to-all(bf16[32,64,384]{2,1,0:T(8,128)(2,1)} %bitcast.117), channel_id=1, replica_groups=mesh['dp'=32,'tensor'=16] {'dp'}, dimensions={0} | all-to-all | bytes 3145728 | tf_op jit(solution)/shard_map/all_to_all | solution.py:94
  496.3 1.3 copy.60
  497.7 58.7 %reduce-scatter.5.cloned.1.call-done = bf16[64,768]{1,0:T(8,128)(2,1)} async-done(((bf16[64,12288]{1,0:T(8,128)(2,1)}), bf16[64,768]{1,0:T(8,128)(2,1)}) %reduce-scatter.5.cloned.1.call-update) | async-done | bytes 98320 | tf_op jit(solution)/shard_map/reduce_scatter | solution.py:95
  556.4 1.6 add_convert_fusion
  (132 shorter events, 5.3 us)
Async XLA Ops:
  6.5 110.9 %copy-start = (bf16[1536]{0:T(1024)(128)(2,1)S(1)}, bf16[1536]{0:T(1024)(128)(2,1)}, u32[]{:S(2)}) copy-start(bf16[1536]{0:T(1024)(128)(2,1)} %param.17) | copy-start | bytes 9220
  6.5 1.9 copy-start.2
  6.5 2.5 copy-start.4
  6.5 2.5 copy-start.5
  11.2 10.4 %copy-start.6 = (s32[64,1,4]{0,2,1:T(4,128)S(1)}, s32[64,1,4]{0,2,1:T(4,128)}, u32[]{:S(2)}) copy-start(s32[64,1,4]{0,2,1:T(4,128)} %param.20) | copy-start | bytes 3076
  11.2 10.5 %copy-start.3 = (bf16[384,1536]{1,0:T(8,128)(2,1)S(1)}, bf16[384,1536]{1,0:T(8,128)(2,1)}, u32[]{:S(2)}) copy-start(bf16[384,1536]{1,0:T(8,128)(2,1)} %param.16) | copy-start | bytes 3538948
  11.2 49.7 %all-to-all-start = ((bf16[64,32,384]{2,0,1:T(8,128)(2,1)}), bf16[64,32,384]{2,0,1:T(8,128)(2,1)}, u32[]{:S(2)}, u32[]{:S(2)}) async-start(bf16[64,32,384]{2,0,1:T(8,128)(2,1)} %bitcast.85), calls=%async_computation | async-start | bytes 3145728 | tf_op jit(solution)/shard_map/all_to_all | solution.py:69
  21.6 315.8 %reduce-scatter.3.cloned.1.call-start = ((), (), s32[]{:S(2)}) async-start(), calls=%async_computation.5 | async-start | bytes 2162688 | tf_op jit(solution)/shard_map/reduce_scatter | solution.py:77
  116.6 0.7 copy-start.8
  339.9 52.9 %all-to-all-start.1 = ((bf16[32,64,512]{2,1,0:T(8,128)(2,1)}), bf16[32,64,512]{2,1,0:T(8,128)(2,1)}, u32[]{:S(2)}, u32[]{:S(2)}) async-start(bf16[32,64,512]{2,1,0:T(8,128)(2,1)} %stack.3), calls=%async_computation.2 | async-start | bytes 4194304 | tf_op jit(solution)/shard_map/all_to_all | solution.py:90
  348.1 208.3 %reduce-scatter.5.cloned.1.call-start = ((), (), s32[]{:S(2)}) async-start(), calls=%async_computation.6 | async-start | bytes 1671168 | tf_op jit(solution)/shard_map/reduce_scatter | solution.py:95
  348.2 48.6 %copy-start.1 = (bf16[1536,384]{1,0:T(8,128)(2,1)S(1)}, bf16[1536,384]{1,0:T(8,128)(2,1)}, u32[]{:S(2)}) copy-start(bf16[1536,384]{1,0:T(8,128)(2,1)} %param.18) | copy-start | bytes 3538948
  496.3 1.4 copy-start.7
Sparse Core Ops, SparseCore 0:
  116.7 220.5 reduce-scatter.2
  497.8 58.5 reduce-scatter.4
